TPU v7x, 32 devices: a whole 2x2x4 slice. The times are simulated.
32 devices in a mesh: groups: 2 (over y), seq: 4 (over z), chan: 4 (over x, core).
Axes of the slice: x: 2, y: 2, z: 4, core: 2. Of those that a mesh axis runs over, the one named last changes fastest.
Arguments:
- value: bfloat16 [1024, 4096], P(('groups', 'seq'), 'chan'), parts along dimension 0, may hold values from -6 to 6
- first_gate: bfloat16 [1024, 4096], P(('groups', 'seq'), 'chan'), parts along dimension 0, may hold values from -6 to 6
- second_gate: bfloat16 [1024, 4096], P(('groups', 'seq'), 'chan'), parts along dimension 0, may hold values from -6 to 6
- first_filter: bfloat16 [256, 512], P('chan'), may hold values from -0.25 to 0.25
- second_filter: bfloat16 [256, 512], P('chan'), may hold values from -0.25 to 0.25
- out_weight: bfloat16 [4096, 4096], P('chan'), may hold values from -0.09375 to 0.09375
- segment_ids: int32 [1024], P(('groups', 'seq')), parts along dimension 0, may hold values from 0 to 1, never falling along the last dimension, each value on 1 to 384 neighbouring positions
Outputs:
- mixed: bfloat16 [1024, 4096], P(('groups', 'seq')), parts along dimension 0
There are 2 independent parts, one for each index of `groups`. A program takes and returns all parts, laid end to end along the dimension named above; an argument that names none is the same for every part. Nothing has to cross between parts.
Inputs may be any that keep to these rules, and one draw needn't show every extreme that they name: `segment_ids`: ids never fall along the window; the 2 contexts each hold 128 to 384 neighbouring positions and together fill the window.
All inputs are finite; a program needn't handle non-finite values.
Results may differ from a plain program's by a relative error of at most 0.0065.
Values may be sent and summed in bfloat16 or wider, within the bound.
A program may use at most 192 MiB of HBM per device.

v0:
```python
import jax
import jax.numpy as jnp
from jax import lax
from jax.sharding import PartitionSpec as P


def toeplitz_taps(doubled, length, base, rows, cols, row_segs, col_segs):
    filt_count = doubled.shape[0]
    span = rows + cols
    start = jnp.mod(base - cols + 1, length)
    window = lax.dynamic_slice_in_dim(doubled, start, span - 1, 1)
    reversed_win = jnp.concatenate(
        [window[:, ::-1], jnp.zeros((filt_count, 1), doubled.dtype)], axis=1
    )
    tiled = jnp.tile(reversed_win, (1, rows))[:, : rows * (span - 1)]
    skewed = tiled.reshape(filt_count, rows, span - 1)[:, :, rows - 1 : rows - 1 + cols]
    same = (row_segs[:, None] == col_segs[None, :]).astype(doubled.dtype)
    return skewed * same[None, :, :]


def apply_taps(grouped, taps):
    return jnp.einsum("gcs,gts->gct", grouped, taps, preferred_element_type=jnp.float32)


def to_rows(result):
    filt_count, per_filter, rows = result.shape
    return result.transpose(2, 0, 1).reshape(rows, filt_count * per_filter)


def local(value, first_gate, second_gate, first_filter, second_filter, out_weight, segment_ids):
    tok_rows = value.shape[0]
    chans = value.shape[1]
    filt_count = first_filter.shape[0]
    length = first_filter.shape[1]
    per_filter = chans // filt_count
    my_start = lax.axis_index("seq") * tok_rows
    seg_row = segment_ids.reshape(1, tok_rows)

    def long_conv(filters, field):
        doubled = jnp.concatenate([filters, filters], axis=1)
        field_cols = field.T
        empty = jnp.zeros((filt_count, per_filter, tok_rows), jnp.float32)
        piece_field = lax.all_gather(field_cols, "seq", axis=1, tiled=True)
        piece_segs = lax.all_gather(seg_row, "seq", axis=1, tiled=True)
        cols = piece_field.shape[1]
        steps_count = cols // tok_rows

        def one_block(index, acc):
            offset = (index * tok_rows).astype(jnp.int32)
            sub_field = lax.dynamic_slice_in_dim(piece_field, offset, tok_rows, 1)
            sub_segs = lax.dynamic_slice_in_dim(piece_segs[0], offset, tok_rows, 0)
            grouped = sub_field.reshape(filt_count, per_filter, tok_rows)
            taps = toeplitz_taps(
                doubled, length, my_start - offset, tok_rows, tok_rows, segment_ids, sub_segs
            )
            return acc + apply_taps(grouped, taps)

        total = lax.fori_loop(0, steps_count, one_block, empty)
        return to_rows(total)

    first_input = (first_gate.astype(jnp.float32) * value.astype(jnp.float32)).astype(jnp.bfloat16)
    first_mix = long_conv(first_filter, first_input)
    second_input = (second_gate.astype(jnp.float32) * first_mix).astype(jnp.bfloat16)
    second_mix = long_conv(second_filter, second_input).astype(jnp.bfloat16)
    partial_out = jnp.dot(second_mix, out_weight, preferred_element_type=jnp.float32)
    mixed = lax.psum(partial_out, "chan").astype(jnp.bfloat16)
    return mixed


def solution(mesh):
    in_specs = (
        P(("groups", "seq"), "chan"),
        P(("groups", "seq"), "chan"),
        P(("groups", "seq"), "chan"),
        P("chan", None),
        P("chan", None),
        P("chan", None),
        P(("groups", "seq")),
    )
    out_specs = P(("groups", "seq"), None)
    return jax.shard_map(local, mesh=mesh, in_specs=in_specs, out_specs=out_specs, check_vma=False)
```

profile of v0, /device:TPU:0, one launch (start us, length us, event | category | flops | bytes accessed | tf_op | source)
XLA Modules:
  0.0 331.8 jit_solution(859946293358869970)
XLA Ops:
  10.8 12.7 %all-gather.1 = s32[4,1,128]{2,1,0:T(1,128)S(1)} all-gather(s32[1,1,128]{2,1,0:T(1,128)} %bitcast.64), channel_id=2, replica_groups=mesh['groups'=2,'seq'=4,'chan'=4] {'seq'}, dimensions={0}, use_global_device_ids=true | all-gather | bytes 2560 | tf_op jit(solution)/shard_map/all_gather | solution.py:44
  24.4 18.2 %all-gather.5.cloned.1.call-done = bf16[1024,512]{1,0:T(8,128)(2,1)} async-done(((bf16[1024,128]{1,0:T(8,128)(2,1)}), bf16[1024,512]{1,0:T(8,128)(2,1)}) %all-gather.5.cloned.1.call-update) | async-done | bytes 1048592 | tf_op jit(solution)/shard_map/all_gather | solution.py:43
  42.6 103.7 %while.36 = (s32[]{:T(128)}, f32[64,16,128]{2,1,0:T(8,128)S(1)}, bf16[1024,512]{1,0:T(8,128)(2,1)}, s32[]{:T(128)}, bf16[64,1024]{1,0:T(8,128)(2,1)S(1)}, /*inde...) while((s32[]{:T(128)}, f32[64,16,128]{2,1,0:T(8,128)S(1)}, ...), condition=%wide.region_1.2_spmd.clone, body=%wide.region_0.1_spmd.clone.sunk | while | flops 34897944 | bytes 33591060 | solution.py:58
  43.3 2.6 copy.21
  48.2 15.8 %reshape.158 = bf16[64,128,255]{2,1,0:T(8,128)(2,1)} reshape(bf16[64,32640]{1,0:T(8,128)(2,1)} %slice.78) | data formatting | bytes 8355840 | tf_op jit(solution)/shard_map/while/body/eval_jaxpr/reshape | solution.py:16
  65.1 3.5 %fusion.23 = f32[64,16,128]{2,1,0:T(8,128)S(1)} fusion(bf16[64,16,128]{2,1,0:T(8,128)(2,1)S(1)} %bitcast.58, bf16[64,128,255]{2,1,0:T(8,128)(2,1)} %reshape.158, bf16[128,128]{1,0:T(8,128)(2,1)S(1)} %compare_convert_fusion.4, f32[64,16,128]{2,1,0:T(8,128)S(1)} %get-tuple-element.645, pred[]{:T(512)S(6)} %compare.16), kind=kOutput, calls=%fused_computation.2.clone.1 | convolution fusion | flops 34865152 | bytes 3440641 | tf_op jit(solution)/shard_map/while/body/eval_jaxpr/gcs,gts->gct/dot_general | solution.py:22
  74.1 15.8 %reshape.158 = bf16[64,128,255]{2,1,0:T(8,128)(2,1)} reshape(bf16[64,32640]{1,0:T(8,128)(2,1)} %slice.78) | data formatting | bytes 8355840 | tf_op jit(solution)/shard_map/while/body/eval_jaxpr/reshape | solution.py:16
  91.0 3.5 %fusion.23 = f32[64,16,128]{2,1,0:T(8,128)S(1)} fusion(bf16[64,16,128]{2,1,0:T(8,128)(2,1)S(1)} %bitcast.58, bf16[64,128,255]{2,1,0:T(8,128)(2,1)} %reshape.158, bf16[128,128]{1,0:T(8,128)(2,1)S(1)} %compare_convert_fusion.4, f32[64,16,128]{2,1,0:T(8,128)S(1)} %get-tuple-element.645, pred[]{:T(512)S(6)} %compare.16), kind=kOutput, calls=%fused_computation.2.clone.1 | convolution fusion | flops 34865152 | bytes 3440641 | tf_op jit(solution)/shard_map/while/body/eval_jaxpr/gcs,gts->gct/dot_general | solution.py:22
  100.0 15.8 %reshape.158 = bf16[64,128,255]{2,1,0:T(8,128)(2,1)} reshape(bf16[64,32640]{1,0:T(8,128)(2,1)} %slice.78) | data formatting | bytes 8355840 | tf_op jit(solution)/shard_map/while/body/eval_jaxpr/reshape | solution.py:16
  117.0 3.5 %fusion.23 = f32[64,16,128]{2,1,0:T(8,128)S(1)} fusion(bf16[64,16,128]{2,1,0:T(8,128)(2,1)S(1)} %bitcast.58, bf16[64,128,255]{2,1,0:T(8,128)(2,1)} %reshape.158, bf16[128,128]{1,0:T(8,128)(2,1)S(1)} %compare_convert_fusion.4, f32[64,16,128]{2,1,0:T(8,128)S(1)} %get-tuple-element.645, pred[]{:T(512)S(6)} %compare.16), kind=kOutput, calls=%fused_computation.2.clone.1 | convolution fusion | flops 34865152 | bytes 3440641 | tf_op jit(solution)/shard_map/while/body/eval_jaxpr/gcs,gts->gct/dot_general | solution.py:22
  126.0 15.8 %reshape.158 = bf16[64,128,255]{2,1,0:T(8,128)(2,1)} reshape(bf16[64,32640]{1,0:T(8,128)(2,1)} %slice.78) | data formatting | bytes 8355840 | tf_op jit(solution)/shard_map/while/body/eval_jaxpr/reshape | solution.py:16
  142.9 3.5 %fusion.23 = f32[64,16,128]{2,1,0:T(8,128)S(1)} fusion(bf16[64,16,128]{2,1,0:T(8,128)(2,1)S(1)} %bitcast.58, bf16[64,128,255]{2,1,0:T(8,128)(2,1)} %reshape.158, bf16[128,128]{1,0:T(8,128)(2,1)S(1)} %compare_convert_fusion.4, f32[64,16,128]{2,1,0:T(8,128)S(1)} %get-tuple-element.645, pred[]{:T(512)S(6)} %compare.16), kind=kOutput, calls=%fused_computation.2.clone.1 | convolution fusion | flops 34865152 | bytes 3440641 | tf_op jit(solution)/shard_map/while/body/eval_jaxpr/gcs,gts->gct/dot_general | solution.py:22
  147.2 28.6 %all-gather.7.cloned.1.call-done = bf16[1024,512]{1,0:T(8,128)(2,1)} async-done(((bf16[1024,128]{1,0:T(8,128)(2,1)}), bf16[1024,512]{1,0:T(8,128)(2,1)}) %all-gather.7.cloned.1.call-update) | async-done | bytes 1048592 | tf_op jit(solution)/shard_map/all_gather | solution.py:43
  175.8 103.7 %while.37 = (s32[]{:T(128)}, f32[64,16,128]{2,1,0:T(8,128)S(1)}, bf16[1024,512]{1,0:T(8,128)(2,1)}, s32[]{:T(128)}, bf16[64,1024]{1,0:T(8,128)(2,1)S(1)}, /*inde...) while((s32[]{:T(128)}, f32[64,16,128]{2,1,0:T(8,128)S(1)}, ...), condition=%wide.region_3.4_spmd.clone, body=%wide.region_2.3_spmd.clone.sunk | while | flops 34897944 | bytes 33591060 | solution.py:58
  181.3 15.8 %reshape.159 = bf16[64,128,255]{2,1,0:T(8,128)(2,1)} reshape(bf16[64,32640]{1,0:T(8,128)(2,1)} %slice.81) | data formatting | bytes 8355840 | tf_op jit(solution)/shard_map/while/body/eval_jaxpr/reshape | solution.py:16
  198.2 3.5 %fusion.26 = f32[64,16,128]{2,1,0:T(8,128)S(1)} fusion(bf16[64,16,128]{2,1,0:T(8,128)(2,1)S(1)} %bitcast.59, bf16[64,128,255]{2,1,0:T(8,128)(2,1)} %reshape.159, bf16[128,128]{1,0:T(8,128)(2,1)S(1)} %compare_convert_fusion.5, f32[64,16,128]{2,1,0:T(8,128)S(1)} %get-tuple-element.690, pred[]{:T(512)S(6)} %compare.17), kind=kOutput, calls=%fused_computation.11.clone.1 | convolution fusion | flops 34865152 | bytes 3440641 | tf_op jit(solution)/shard_map/while/body/eval_jaxpr/gcs,gts->gct/dot_general | solution.py:22
  207.3 15.8 %reshape.159 = bf16[64,128,255]{2,1,0:T(8,128)(2,1)} reshape(bf16[64,32640]{1,0:T(8,128)(2,1)} %slice.81) | data formatting | bytes 8355840 | tf_op jit(solution)/shard_map/while/body/eval_jaxpr/reshape | solution.py:16
  224.2 3.5 %fusion.26 = f32[64,16,128]{2,1,0:T(8,128)S(1)} fusion(bf16[64,16,128]{2,1,0:T(8,128)(2,1)S(1)} %bitcast.59, bf16[64,128,255]{2,1,0:T(8,128)(2,1)} %reshape.159, bf16[128,128]{1,0:T(8,128)(2,1)S(1)} %compare_convert_fusion.5, f32[64,16,128]{2,1,0:T(8,128)S(1)} %get-tuple-element.690, pred[]{:T(512)S(6)} %compare.17), kind=kOutput, calls=%fused_computation.11.clone.1 | convolution fusion | flops 34865152 | bytes 3440641 | tf_op jit(solution)/shard_map/while/body/eval_jaxpr/gcs,gts->gct/dot_general | solution.py:22
  233.2 15.8 %reshape.159 = bf16[64,128,255]{2,1,0:T(8,128)(2,1)} reshape(bf16[64,32640]{1,0:T(8,128)(2,1)} %slice.81) | data formatting | bytes 8355840 | tf_op jit(solution)/shard_map/while/body/eval_jaxpr/reshape | solution.py:16
  250.1 3.5 %fusion.26 = f32[64,16,128]{2,1,0:T(8,128)S(1)} fusion(bf16[64,16,128]{2,1,0:T(8,128)(2,1)S(1)} %bitcast.59, bf16[64,128,255]{2,1,0:T(8,128)(2,1)} %reshape.159, bf16[128,128]{1,0:T(8,128)(2,1)S(1)} %compare_convert_fusion.5, f32[64,16,128]{2,1,0:T(8,128)S(1)} %get-tuple-element.690, pred[]{:T(512)S(6)} %compare.17), kind=kOutput, calls=%fused_computation.11.clone.1 | convolution fusion | flops 34865152 | bytes 3440641 | tf_op jit(solution)/shard_map/while/body/eval_jaxpr/gcs,gts->gct/dot_general | solution.py:22
  259.1 15.8 %reshape.159 = bf16[64,128,255]{2,1,0:T(8,128)(2,1)} reshape(bf16[64,32640]{1,0:T(8,128)(2,1)} %slice.81) | data formatting | bytes 8355840 | tf_op jit(solution)/shard_map/while/body/eval_jaxpr/reshape | solution.py:16
  276.1 3.5 %fusion.26 = f32[64,16,128]{2,1,0:T(8,128)S(1)} fusion(bf16[64,16,128]{2,1,0:T(8,128)(2,1)S(1)} %bitcast.59, bf16[64,128,255]{2,1,0:T(8,128)(2,1)} %reshape.159, bf16[128,128]{1,0:T(8,128)(2,1)S(1)} %compare_convert_fusion.5, f32[64,16,128]{2,1,0:T(8,128)S(1)} %get-tuple-element.690, pred[]{:T(512)S(6)} %compare.17), kind=kOutput, calls=%fused_computation.11.clone.1 | convolution fusion | flops 34865152 | bytes 3440641 | tf_op jit(solution)/shard_map/while/body/eval_jaxpr/gcs,gts->gct/dot_general | solution.py:22
  279.6 4.7 %fusion.10 = f32[128,4096]{1,0:T(8,128)S(1)} fusion(bf16[128,1024]{0,1:T(8,128)(2,1)S(1)} %bitcast.62, bf16[1024,4096]{1,0:T(8,128)(2,1)} %param.16), kind=kOutput, calls=%fused_computation.24 | convolution fusion | flops 1073741824 | bytes 10747904 | tf_op jit(solution)/shard_map/dot_general | solution.py:65
  284.2 40.7 %all-reduce.3 = bf16[128,4096]{1,0:T(8,128)(2,1)} all-reduce(f32[128,4096]{1,0:T(8,128)S(1)} %fusion.10), channel_id=1, replica_groups=mesh['groups'=2,'seq'=4,'chan'=4] {'chan'}, use_global_device_ids=true, to_apply=%region_4.5 | all-reduce | flops 524288 | bytes 3145728 | tf_op jit(solution)/shard_map/psum | solution.py:66
  (111 shorter events, 55.9 us)
Async XLA Ops:
  6.5 36.1 %all-gather.5.cloned.1.call-start = ((), (), s32[]{:S(2)}) async-start(), calls=%async_computation | async-start | bytes 1310720 | tf_op jit(solution)/shard_map/all_gather | solution.py:43
  9.6 166.2 %all-gather.7.cloned.1.call-start = ((), (), s32[]{:S(2)}) async-start(), calls=%async_computation.1 | async-start | bytes 1310720 | tf_op jit(solution)/shard_map/all_gather | solution.py:43
  42.6 104.5 %copy-start = (bf16[64,512]{1,0:T(8,128)(2,1)S(1)}, bf16[64,512]{1,0:T(8,128)(2,1)}, u32[]{:S(2)}) copy-start(bf16[64,512]{1,0:T(8,128)(2,1)} %param.15) | copy-start | bytes 196612
  48.2 15.8 %copy-start.1 = (s32[128]{0:T(128)S(1)}, s32[128]{0:T(128)}, u32[]{:S(2)}) copy-start(s32[128]{0:T(128)} %get-tuple-element.664) | copy-start | bytes 1540 | tf_op jit(solution)/shard_map/while
  74.1 15.8 %copy-start.1 = (s32[128]{0:T(128)S(1)}, s32[128]{0:T(128)}, u32[]{:S(2)}) copy-start(s32[128]{0:T(128)} %get-tuple-element.664) | copy-start | bytes 1540 | tf_op jit(solution)/shard_map/while
  100.0 15.8 %copy-start.1 = (s32[128]{0:T(128)S(1)}, s32[128]{0:T(128)}, u32[]{:S(2)}) copy-start(s32[128]{0:T(128)} %get-tuple-element.664) | copy-start | bytes 1540 | tf_op jit(solution)/shard_map/while
  126.0 15.8 %copy-start.1 = (s32[128]{0:T(128)S(1)}, s32[128]{0:T(128)}, u32[]{:S(2)}) copy-start(s32[128]{0:T(128)} %get-tuple-element.664) | copy-start | bytes 1540 | tf_op jit(solution)/shard_map/while
  181.3 15.8 %copy-start.2 = (s32[128]{0:T(128)S(1)}, s32[128]{0:T(128)}, u32[]{:S(2)}) copy-start(s32[128]{0:T(128)} %get-tuple-element.709) | copy-start | bytes 1540 | tf_op jit(solution)/shard_map/while
  207.3 15.8 %copy-start.2 = (s32[128]{0:T(128)S(1)}, s32[128]{0:T(128)}, u32[]{:S(2)}) copy-start(s32[128]{0:T(128)} %get-tuple-element.709) | copy-start | bytes 1540 | tf_op jit(solution)/shard_map/while
  233.2 15.8 %copy-start.2 = (s32[128]{0:T(128)S(1)}, s32[128]{0:T(128)}, u32[]{:S(2)}) copy-start(s32[128]{0:T(128)} %get-tuple-element.709) | copy-start | bytes 1540 | tf_op jit(solution)/shard_map/while
  259.1 15.8 %copy-start.2 = (s32[128]{0:T(128)S(1)}, s32[128]{0:T(128)}, u32[]{:S(2)}) copy-start(s32[128]{0:T(128)} %get-tuple-element.709) | copy-start | bytes 1540 | tf_op jit(solution)/shard_map/while
Sparse Core Ops, SparseCore 0:
  9.7 32.8 all-gather.4
  147.3 28.4 all-gather.6
where the time goes:
time: 333 us; the launch traced here: 332 us
  local copies, waits for them, and re-layouts  182 us (55%)
  blocking collectives  53.4 us (16%)
  waiting for transfers between devices  46.9 us (14%)
  matrix products  32.3 us (10%)
  between operations  13.5 us (4%)
    reshape x8, local copies, waits for them, and re-layouts, toeplitz_taps(): tiled.reshape(filt_count, rows, span - 1)[:, :, rows - 1:rows - 1 + cols]  127 us
    all_gather x2, waiting for transfers between devices, long_conv(): piece_field = lax.all_gather(field_cols, 'seq', axis=1, tiled=True)  46.8 us
    psum x1, blocking collectives, local(): mixed = lax.psum(partial_out, 'chan').astype(jnp.bfloat16)  40.7 us
    dot_general x8, matrix products, apply_taps(): jnp.einsum('gcs,gts->gct', grouped, taps, preferred_element_type=jnp.floa...  27.7 us
    while x40, local copies, waits for them, and re-layouts  23 us
    slice x8, local copies, waits for them, and re-layouts, toeplitz_taps(): tiled = jnp.tile(reversed_win, (1, rows))[:, :rows * (span - 1)]  18 us
    all_gather x1, blocking collectives, long_conv(): piece_segs = lax.all_gather(seg_row, 'seq', axis=1, tiled=True)  12.7 us
    dynamic_slice x8, local copies, waits for them, and re-layouts, one_block(): sub_field = lax.dynamic_slice_in_dim(piece_field, offset, tok_rows, 1)  7.8 us
  transfers between devices with their start and end apart: 2, of which 2 were waited for; matrix products, arithmetic and copies ran while one was open for 1% of the time, Pallas kernels for 0%

commit v1 on v0

v1 whole, which is shorter than its diff:
```python
import functools

import jax
import jax.numpy as jnp
from jax import lax
from jax.experimental import pallas as pl
from jax.experimental.pallas import tpu as pltpu
from jax.sharding import PartitionSpec as P

MESH = pl.DeviceIdType.MESH
TILE = 256
LANES = 128
CORES = 2


def remote(src, dst, send, recv, where):
    return pltpu.make_async_remote_copy(
        src_ref=src, dst_ref=dst, send_sem=send, recv_sem=recv, device_id=where, device_id_type=MESH
    )


def kernel(
    seqs, chans, chunks,
    value, gate1, gate2, filt1, filt2, weight, segs,
    out,
    taps_f32, taps, z_send, z_recv, g_send, g_recv, seg_all, mix, m_send, m_recv,
    w_buf, p_send, p_recv, x_buf,
    w_sem, z_ss, z_rs, g_ss, g_rs, s_ss, s_rs, m_ss, m_rs, p_ss, p_rs, x_ss, x_rs, o_ss, o_rs,
):
    me = lax.axis_index("seq")
    chan = lax.axis_index("chan")
    chips = chans // CORES
    core = lax.rem(chan, CORES)
    chip = lax.div(chan, CORES)
    partner = chip * CORES + (1 - core)
    tok = value.shape[0]
    length = filt1.shape[1]
    mine_filts = taps.shape[1]
    rows = z_send.shape[1]
    per = rows // mine_filts
    blocks = length // TILE
    half_cols = weight.shape[1] // CORES
    width = half_cols // chunks

    seq_peers = [lax.rem(me + d, seqs) for d in range(1, seqs)]
    chip_peers = [lax.rem(chip + d, chips) * CORES + core for d in range(1, chips)]

    barrier = pltpu.get_barrier_semaphore()
    for peer in seq_peers:
        pl.semaphore_signal(barrier, inc=1, device_id={"seq": peer}, device_id_type=MESH)
    for peer in chip_peers + [partner]:
        pl.semaphore_signal(barrier, inc=1, device_id={"chan": peer}, device_id_type=MESH)

    w_copies = []
    for side in range(CORES):
        owner = 1 - core if side == 0 else core
        for q in range(chunks):
            at = pl.multiple_of(owner * half_cols + q * width, width)
            copy = pltpu.make_async_copy(
                weight.at[:, pl.ds(at, width)], w_buf.at[side, q], w_sem.at[side, q]
            )
            copy.start()
            w_copies.append(copy)

    prod = (gate1[...].astype(jnp.float32) * value[...].astype(jnp.float32)).astype(jnp.bfloat16)
    z_send[...] = prod.T.reshape(seqs, rows, tok)

    pl.semaphore_wait(barrier, seqs - 1 + chips)

    copies = []
    for d, peer in enumerate(seq_peers):
        copy = remote(segs, seg_all.at[me], s_ss.at[d], s_rs.at[d], {"seq": peer})
        copy.start()
        copies.append(copy)
    for d, peer in enumerate(seq_peers):
        copy = remote(z_send.at[peer], z_recv.at[me], z_ss.at[d], z_rs.at[d], {"seq": peer})
        copy.start()
        copies.append(copy)
    g_send[...] = gate2[...].T.reshape(seqs, rows, tok)
    g_copies = []
    for d, peer in enumerate(seq_peers):
        copy = remote(g_send.at[peer], g_recv.at[me], g_ss.at[d], g_rs.at[d], {"seq": peer})
        copy.start()
        g_copies.append(copy)
    seg_all[me] = segs[...]
    z_recv[me] = z_send[me]
    g_recv[me] = g_send[me]

    for which, filt in enumerate((filt1, filt2)):
        taps_f32[which] = filt[...].astype(jnp.float32)

        def build(f, carry):
            row = taps_f32[which, pl.ds(me * mine_filts + f, 1), :]
            wide = jnp.broadcast_to(row, (LANES, length))
            low = pltpu.roll(wide, 0, 1, stride=1, stride_axis=0).astype(jnp.bfloat16)
            taps[which, f, pl.ds(0, LANES), :] = low
            taps[which, f, pl.ds(LANES, LANES), :] = jnp.concatenate(
                [low[:, length - LANES :], low[:, : length - LANES]], axis=1
            )
            return carry

        lax.fori_loop(0, mine_filts, build, 0)

    for copy in copies:
        copy.wait_recv()

    ids = jnp.concatenate([seg_all[j] for j in range(seqs)], axis=1)
    first = jnp.broadcast_to((ids == 0).astype(jnp.float32), (per, length))
    in_first = first > 0.5
    keep = (first.astype(jnp.bfloat16), (1.0 - first).astype(jnp.bfloat16))

    def conv(which, f, field):
        parts = []
        for j in range(blocks):
            span = slice(j * TILE, (j + 1) * TILE)
            parts += [field[:, span] * keep[0][:, span], field[:, span] * keep[1][:, span]]
        lhs = jnp.concatenate(parts, axis=0)
        res = jnp.dot(lhs, taps[which, f], preferred_element_type=jnp.float32)
        sums = []
        for context in range(2):
            total = None
            for j in range(blocks):
                at = (2 * j + context) * per
                piece = res[at : at + per]
                if j:
                    cut = length - j * TILE
                    piece = jnp.concatenate([piece[:, cut:], piece[:, :cut]], axis=1)
                total = piece if total is None else total + piece
            sums.append(total)
        return jnp.where(in_first, sums[0], sums[1])

    def rows_of(f):
        return pl.ds(pl.multiple_of(f * per, per), per)

    def first_conv(f, carry):
        field = jnp.concatenate([z_recv[j, rows_of(f), :] for j in range(seqs)], axis=1)
        mix[rows_of(f), :] = conv(0, f, field)
        return carry

    lax.fori_loop(0, mine_filts, first_conv, 0)

    for copy in g_copies:
        copy.wait_recv()

    def second_conv(f, carry):
        gate = jnp.concatenate([g_recv[j, rows_of(f), :] for j in range(seqs)], axis=1)
        field = (gate.astype(jnp.float32) * mix[rows_of(f), :]).astype(jnp.bfloat16)
        result = conv(1, f, field).astype(jnp.bfloat16)
        for j in range(seqs):
            m_send[j, rows_of(f), :] = result[:, j * tok : (j + 1) * tok]
        return carry

    lax.fori_loop(0, mine_filts, second_conv, 0)

    m_copies = []
    for d, peer in enumerate(seq_peers):
        copy = remote(m_send.at[peer], m_recv.at[me], m_ss.at[d], m_rs.at[d], {"seq": peer})
        copy.start()
        m_copies.append(copy)
    m_recv[me] = m_send[me]
    for copy in w_copies:
        copy.wait()
    for copy in m_copies:
        copy.wait_recv()

    lhs = m_recv[...].reshape(seqs * rows, tok).T
    p_copies = []
    for q in range(chunks):
        p_send[q] = jnp.dot(lhs, w_buf[0, q], preferred_element_type=jnp.float32).astype(jnp.bfloat16)
        copy = remote(p_send.at[q], p_recv.at[q], p_ss.at[q], p_rs.at[q], {"chan": partner})
        copy.start()
        p_copies.append(copy)
    x_copies = []
    for q in range(chunks):
        part = jnp.dot(lhs, w_buf[1, q], preferred_element_type=jnp.float32)
        p_copies[q].wait_recv()
        x_buf[chip, q] = (part + p_recv[q].astype(jnp.float32)).astype(jnp.bfloat16)
        x_copies.append([])
        for d, peer in enumerate(chip_peers):
            copy = remote(x_buf.at[chip, q], x_buf.at[chip, q], x_ss.at[q, d], x_rs.at[q, d], {"chan": peer})
            copy.start()
            x_copies[q].append(copy)
    o_copies = []
    for q in range(chunks):
        for copy in x_copies[q]:
            copy.wait_recv()
        total = x_buf[0, q].astype(jnp.float32)
        for j in range(1, chips):
            total = total + x_buf[j, q].astype(jnp.float32)
        here = out.at[:, pl.ds(pl.multiple_of(core * half_cols + q * width, width), width)]
        here[...] = total.astype(jnp.bfloat16)
        copy = remote(here, here, o_ss.at[q], o_rs.at[q], {"chan": partner})
        copy.start()
        o_copies.append(copy)
    for copy in copies + g_copies + m_copies + p_copies + [c for cs in x_copies for c in cs]:
        copy.wait_send()
    for copy in o_copies:
        copy.wait()


def local(seqs, chans, value, gate1, gate2, filt1, filt2, weight, segs):
    tok, width = value.shape
    filts, length = filt1.shape
    cols = weight.shape[1]
    chips = chans // CORES
    chunks = 4
    chunk = cols // CORES // chunks
    mine = filts // seqs
    rows = width // seqs
    bf16, f32 = jnp.bfloat16, jnp.float32
    dma = pltpu.SemaphoreType.DMA
    others = seqs - 1
    vmem = pl.BlockSpec(memory_space=pltpu.VMEM)
    return pl.pallas_call(
        functools.partial(kernel, seqs, chans, chunks),
        out_shape=jax.ShapeDtypeStruct((tok, cols), bf16),
        in_specs=[vmem] * 5 + [pl.BlockSpec(memory_space=pl.ANY), vmem],
        out_specs=vmem,
        scratch_shapes=[
            pltpu.VMEM((2, filts, length), f32),
            pltpu.VMEM((2, mine, TILE, length), bf16),
            pltpu.VMEM((seqs, rows, tok), bf16),
            pltpu.VMEM((seqs, rows, tok), bf16),
            pltpu.VMEM((seqs, rows, tok), bf16),
            pltpu.VMEM((seqs, rows, tok), bf16),
            pltpu.VMEM((seqs, 1, tok), jnp.int32),
            pltpu.VMEM((rows, length), f32),
            pltpu.VMEM((seqs, rows, tok), bf16),
            pltpu.VMEM((seqs, rows, tok), bf16),
            pltpu.VMEM((CORES, chunks, width, chunk), bf16),
            pltpu.VMEM((chunks, tok, chunk), bf16),
            pltpu.VMEM((chunks, tok, chunk), bf16),
            pltpu.VMEM((chips, chunks, tok, chunk), bf16),
            dma((CORES, chunks)),
            dma((others,)), dma((others,)), dma((others,)), dma((others,)),
            dma((others,)), dma((others,)), dma((others,)), dma((others,)),
            dma((chunks,)), dma((chunks,)),
            dma((chunks, chips - 1)), dma((chunks, chips - 1)),
            dma((chunks,)), dma((chunks,)),
        ],
        compiler_params=pltpu.CompilerParams(
            collective_id=0, has_side_effects=True, vmem_limit_bytes=48 * 1024 * 1024
        ),
    )(value, gate1, gate2, filt1, filt2, weight, segs.reshape(1, tok))


def solution(mesh):
    in_specs = (
        P(("groups", "seq"), "chan"),
        P(("groups", "seq"), "chan"),
        P(("groups", "seq"), "chan"),
        P("chan", None),
        P("chan", None),
        P("chan", None),
        P(("groups", "seq")),
    )
    out_specs = P(("groups", "seq"), None)
    body = functools.partial(local, mesh.shape["seq"], mesh.shape["chan"])
    return jax.shard_map(body, mesh=mesh, in_specs=in_specs, out_specs=out_specs, check_vma=False)
```

time: 333 us -> 49.2 us (0.15)
  local copies, waits for them, and re-layouts: 182 us -> 6.15 us
  blocking collectives: 53.4 us -> 0 us
  waiting for transfers between devices: 46.9 us -> 0 us
  Pallas kernels: 0 us -> 42.7 us
  matrix products: 32.3 us -> 0 us
  between operations: 13.5 us -> 0.02 us
    reshape x8 -> x0, local copies, waits for them, and re-layouts: 127 us -> none  [toeplitz_taps(): tiled.reshape(filt_count, rows, span - 1)[:, :, rows - 1:rows - 1 + cols]]
    all_gather x2 -> x0, waiting for transfers between devices: 46.8 us -> none  [long_conv(): piece_field = lax.all_gather(field_cols, 'seq', axis=1, tiled=True)]
    pallas_call x0 -> x1, Pallas kernels: none -> 42.7 us  [local(): pl.pallas_call(functools.partial(kernel, seqs, chans, chunks), out_shape=...]
    psum x1 -> x0, blocking collectives: 40.7 us -> none  [local(): mixed = lax.psum(partial_out, 'chan').astype(jnp.bfloat16)]
    dot_general x9 -> x0, matrix products: 32.3 us -> none  [the longest x8 27.7 us: apply_taps(): jnp.einsum('gcs,gts->gct', grouped, taps, preferred_element_type=jnp.floa...]
    while x40 -> x0, local copies, waits for them, and re-layouts: 23 us -> none
    slice x8 -> x0, local copies, waits for them, and re-layouts: 18 us -> none  [toeplitz_taps(): tiled = jnp.tile(reversed_win, (1, rows))[:, :rows * (span - 1)]]
    all_gather x1 -> x0, blocking collectives: 12.7 us -> none  [long_conv(): piece_segs = lax.all_gather(seg_row, 'seq', axis=1, tiled=True)]
  transfers between devices with their start and end apart: 2 -> 0, of which waited for: 2 -> 0; matrix products, arithmetic and copies ran while one was open for 1% -> 0% of each run, Pallas kernels for 0% -> 0%
where the time goes in v1:
time: 49.2 us; the launch traced here: 48.9 us
  Pallas kernels  42.7 us (87%)
  local copies, waits for them, and re-layouts  6.15 us (12%)
    pallas_call x1, Pallas kernels, local(): pl.pallas_call(functools.partial(kernel, seqs, chans, chunks), out_shape=...  42.7 us
    unnamed x13, local copies, waits for them, and re-layouts  6.15 us

profile of v1, /device:TPU:0, one launch (start us, length us, event | category | flops | bytes accessed | tf_op | source)
XLA Modules:
  0.0 48.9 jit_solution(14932679864390944147)
XLA Ops:
  0.0 0.0 copy-start
  0.0 0.9 %copy-done = bf16[128,1024]{1,0:T(8,128)(2,1)S(1)} copy-done((bf16[128,1024]{1,0:T(8,128)(2,1)S(1)}, bf16[128,1024]{1,0:T(8,128)(2,1)}, u32[]{:S(2)}) %copy-start) | copy-done | bytes 262168
  1.0 0.0 copy-start.1
  1.0 0.9 %copy-done.1 = bf16[128,1024]{1,0:T(8,128)(2,1)S(1)} copy-done((bf16[128,1024]{1,0:T(8,128)(2,1)S(1)}, bf16[128,1024]{1,0:T(8,128)(2,1)}, u32[]{:S(2)}) %copy-start.1) | copy-done | bytes 262168
  1.9 0.0 copy-start.2
  1.9 0.9 %copy-done.2 = bf16[128,1024]{1,0:T(8,128)(2,1)S(1)} copy-done((bf16[128,1024]{1,0:T(8,128)(2,1)S(1)}, bf16[128,1024]{1,0:T(8,128)(2,1)}, u32[]{:S(2)}) %copy-start.2) | copy-done | bytes 262168
  2.9 0.0 copy-start.3
  2.9 0.8 %copy-done.3 = bf16[64,512]{1,0:T(8,128)(2,1)S(1)} copy-done((bf16[64,512]{1,0:T(8,128)(2,1)S(1)}, bf16[64,512]{1,0:T(8,128)(2,1)}, u32[]{:S(2)}) %copy-start.3) | copy-done | bytes 65560
  3.7 0.0 copy-start.4
  3.7 0.8 %copy-done.4 = bf16[64,512]{1,0:T(8,128)(2,1)S(1)} copy-done((bf16[64,512]{1,0:T(8,128)(2,1)S(1)}, bf16[64,512]{1,0:T(8,128)(2,1)}, u32[]{:S(2)}) %copy-start.4) | copy-done | bytes 65560
  4.5 0.0 copy-start.5
  4.5 0.7 %copy-done.5 = s32[128]{0:T(128)S(1)} copy-done((s32[128]{0:T(128)S(1)}, s32[128]{0:T(128)}, u32[]{:S(2)}) %copy-start.5) | copy-done | bytes 536
  5.2 42.7 %shard_map.73 = bf16[128,4096]{1,0:T(8,128)(2,1)S(1)} custom-call(bf16[128,1024]{1,0:T(8,128)(2,1)S(1)} %copy-done, bf16[128,1024]{1,0:T(8,128)(2,1)S(1)} %copy-done.1, bf16[128,1024]{1,0:T(8,128)(2,1)S(1)} %copy-done.2, bf16[64,512]{1,0:T(8,128)(2,1)S(1)} %copy-done.3, bf16[64,512]{1,0:T(8,128)(2,1)S(1)} %copy-done.4, bf16[1024,4096]{1,0:T(8,128)(2,1)} %weight.1, ...), custom_call_target="tpu_custom_call" | custom-call | tf_op jit(solution)/shard_map/pallas_call | solution.py:214
  47.9 1.0 %copy.9 = bf16[128,4096]{1,0:T(8,128)(2,1)} copy(bf16[128,4096]{1,0:T(8,128)(2,1)S(1)} %shard_map.73) | data formatting | bytes 2097152
Async XLA Ops:
  0.0 0.9 %copy-start = (bf16[128,1024]{1,0:T(8,128)(2,1)S(1)}, bf16[128,1024]{1,0:T(8,128)(2,1)}, u32[]{:S(2)}) copy-start(bf16[128,1024]{1,0:T(8,128)(2,1)} %value.1) | copy-start | bytes 786436
  1.0 0.9 %copy-start.1 = (bf16[128,1024]{1,0:T(8,128)(2,1)S(1)}, bf16[128,1024]{1,0:T(8,128)(2,1)}, u32[]{:S(2)}) copy-start(bf16[128,1024]{1,0:T(8,128)(2,1)} %gate1.1) | copy-start | bytes 786436
  1.9 0.9 %copy-start.2 = (bf16[128,1024]{1,0:T(8,128)(2,1)S(1)}, bf16[128,1024]{1,0:T(8,128)(2,1)}, u32[]{:S(2)}) copy-start(bf16[128,1024]{1,0:T(8,128)(2,1)} %gate2.1) | copy-start | bytes 786436
  2.9 0.8 %copy-start.3 = (bf16[64,512]{1,0:T(8,128)(2,1)S(1)}, bf16[64,512]{1,0:T(8,128)(2,1)}, u32[]{:S(2)}) copy-start(bf16[64,512]{1,0:T(8,128)(2,1)} %filt1.1) | copy-start | bytes 196612
  3.7 0.8 %copy-start.4 = (bf16[64,512]{1,0:T(8,128)(2,1)S(1)}, bf16[64,512]{1,0:T(8,128)(2,1)}, u32[]{:S(2)}) copy-start(bf16[64,512]{1,0:T(8,128)(2,1)} %filt2.1) | copy-start | bytes 196612
  4.5 0.7 %copy-start.5 = (s32[128]{0:T(128)S(1)}, s32[128]{0:T(128)}, u32[]{:S(2)}) copy-start(s32[128]{0:T(128)} %param.13) | copy-start | bytes 1540

commit v2 on v1

--- a/solution.py
+++ b/solution.py
@@ -1,4 +1,5 @@
 import functools
+import math
 
 import jax
 import jax.numpy as jnp
@@ -11,6 +12,8 @@
 TILE = 256
 LANES = 128
 CORES = 2
+GROUP = 4
+PARTS = 2
 
 
 def remote(src, dst, send, recv, where):
@@ -21,11 +24,12 @@
 
 def kernel(
     seqs, chans, chunks,
-    value, gate1, gate2, filt1, filt2, weight, segs,
+    value_in, gate1_in, gate2_in, filt1_in, filt2_in, weight, segs_in,
     out,
+    value, gate1, gate2, filt1, filt2, segs,
     taps_f32, taps, z_send, z_recv, g_send, g_recv, seg_all, mix, m_send, m_recv,
     w_buf, p_send, p_recv, x_buf,
-    w_sem, z_ss, z_rs, g_ss, g_rs, s_ss, s_rs, m_ss, m_rs, p_ss, p_rs, x_ss, x_rs, o_ss, o_rs,
+    i_sem, w_sem, z_ss, z_rs, g_ss, g_rs, s_ss, s_rs, m_ss, m_rs, p_ss, p_rs, x_ss, x_rs, o_ss, o_rs,
 ):
     me = lax.axis_index("seq")
     chan = lax.axis_index("chan")
@@ -39,6 +43,10 @@
     rows = z_send.shape[1]
     per = rows // mine_filts
     blocks = length // TILE
+    parts = z_ss.shape[0]
+    part_filts = mine_filts // parts
+    part_rows = rows // parts
+    step = math.gcd(part_filts, GROUP)
     half_cols = weight.shape[1] // CORES
     width = half_cols // chunks
 
@@ -50,6 +58,13 @@
         pl.semaphore_signal(barrier, inc=1, device_id={"seq": peer}, device_id_type=MESH)
     for peer in chip_peers + [partner]:
         pl.semaphore_signal(barrier, inc=1, device_id={"chan": peer}, device_id_type=MESH)
+
+    ins = []
+    pairs = ((value_in, value), (gate1_in, gate1), (gate2_in, gate2), (filt1_in, filt1), (filt2_in, filt2), (segs_in, segs))
+    for index, (source, target) in enumerate(pairs):
+        copy = pltpu.make_async_copy(source, target, i_sem.at[index])
+        copy.start()
+        ins.append(copy)
 
     w_copies = []
     for side in range(CORES):
@@ -62,31 +77,42 @@
             copy.start()
             w_copies.append(copy)
 
+    ins[0].wait()
+    ins[1].wait()
     prod = (gate1[...].astype(jnp.float32) * value[...].astype(jnp.float32)).astype(jnp.bfloat16)
     z_send[...] = prod.T.reshape(seqs, rows, tok)
 
     pl.semaphore_wait(barrier, seqs - 1 + chips)
 
-    copies = []
+    def exchange(source, target, sends, recvs, part):
+        span = pl.ds(part * part_rows, part_rows)
+        started = []
+        for d, peer in enumerate(seq_peers):
+            copy = remote(
+                source.at[peer, span], target.at[me, span], sends.at[part, d], recvs.at[part, d], {"seq": peer}
+            )
+            copy.start()
+            started.append(copy)
+        return started
+
+    ins[5].wait()
+    s_copies = []
     for d, peer in enumerate(seq_peers):
         copy = remote(segs, seg_all.at[me], s_ss.at[d], s_rs.at[d], {"seq": peer})
         copy.start()
-        copies.append(copy)
-    for d, peer in enumerate(seq_peers):
-        copy = remote(z_send.at[peer], z_recv.at[me], z_ss.at[d], z_rs.at[d], {"seq": peer})
-        copy.start()
-        copies.append(copy)
+        s_copies.append(copy)
+    z_copies = [exchange(z_send, z_recv, z_ss, z_rs, 0)]
+    ins[2].wait()
     g_send[...] = gate2[...].T.reshape(seqs, rows, tok)
-    g_copies = []
-    for d, peer in enumerate(seq_peers):
-        copy = remote(g_send.at[peer], g_recv.at[me], g_ss.at[d], g_rs.at[d], {"seq": peer})
-        copy.start()
-        g_copies.append(copy)
+    g_copies = [exchange(g_send, g_recv, g_ss, g_rs, 0)]
+    for part in range(1, parts):
+        z_copies.append(exchange(z_send, z_recv, z_ss, z_rs, part))
+        g_copies.append(exchange(g_send, g_recv, g_ss, g_rs, part))
     seg_all[me] = segs[...]
     z_recv[me] = z_send[me]
     g_recv[me] = g_send[me]
 
-    for which, filt in enumerate((filt1, filt2)):
+    def build_taps(which, filt):
         taps_f32[which] = filt[...].astype(jnp.float32)
 
         def build(f, carry):
@@ -101,7 +127,11 @@
 
         lax.fori_loop(0, mine_filts, build, 0)
 
-    for copy in copies:
+    ins[3].wait()
+    ins[4].wait()
+    build_taps(0, filt1)
+
+    for copy in s_copies:
         copy.wait_recv()
 
     ids = jnp.concatenate([seg_all[j] for j in range(seqs)], axis=1)
@@ -132,31 +162,38 @@
     def rows_of(f):
         return pl.ds(pl.multiple_of(f * per, per), per)
 
-    def first_conv(f, carry):
-        field = jnp.concatenate([z_recv[j, rows_of(f), :] for j in range(seqs)], axis=1)
-        mix[rows_of(f), :] = conv(0, f, field)
+    def joined(ref, f):
+        return jnp.concatenate([ref[j, rows_of(f), :] for j in range(seqs)], axis=1)
+
+    def first_conv(base, i, carry):
+        at = [base + i * step + k for k in range(step)]
+        fields = [joined(z_recv, f) for f in at]
+        results = [conv(0, f, field) for f, field in zip(at, fields)]
+        for f, result in zip(at, results):
+            mix[rows_of(f), :] = result
         return carry
 
-    lax.fori_loop(0, mine_filts, first_conv, 0)
-
-    for copy in g_copies:
-        copy.wait_recv()
-
-    def second_conv(f, carry):
-        gate = jnp.concatenate([g_recv[j, rows_of(f), :] for j in range(seqs)], axis=1)
-        field = (gate.astype(jnp.float32) * mix[rows_of(f), :]).astype(jnp.bfloat16)
-        result = conv(1, f, field).astype(jnp.bfloat16)
-        for j in range(seqs):
-            m_send[j, rows_of(f), :] = result[:, j * tok : (j + 1) * tok]
+    def second_conv(base, i, carry):
+        at = [base + i * step + k for k in range(step)]
+        fields = [(joined(g_recv, f).astype(jnp.float32) * mix[rows_of(f), :]).astype(jnp.bfloat16) for f in at]
+        results = [conv(1, f, field).astype(jnp.bfloat16) for f, field in zip(at, fields)]
+        for f, result in zip(at, results):
+            for j in range(seqs):
+                m_send[j, rows_of(f), :] = result[:, j * tok : (j + 1) * tok]
         return carry
 
-    lax.fori_loop(0, mine_filts, second_conv, 0)
-
     m_copies = []
-    for d, peer in enumerate(seq_peers):
-        copy = remote(m_send.at[peer], m_recv.at[me], m_ss.at[d], m_rs.at[d], {"seq": peer})
-        copy.start()
-        m_copies.append(copy)
+    for part in range(parts):
+        base = part * part_filts
+        for copy in z_copies[part]:
+            copy.wait_recv()
+        lax.fori_loop(0, part_filts // step, functools.partial(first_conv, base), 0)
+        if part == 0:
+            build_taps(1, filt2)
+        for copy in g_copies[part]:
+            copy.wait_recv()
+        lax.fori_loop(0, part_filts // step, functools.partial(second_conv, base), 0)
+        m_copies += exchange(m_send, m_recv, m_ss, m_rs, part)
     m_recv[me] = m_send[me]
     for copy in w_copies:
         copy.wait()
@@ -192,7 +229,8 @@
         copy = remote(here, here, o_ss.at[q], o_rs.at[q], {"chan": partner})
         copy.start()
         o_copies.append(copy)
-    for copy in copies + g_copies + m_copies + p_copies + [c for cs in x_copies for c in cs]:
+    nested = [c for cs in z_copies + g_copies + x_copies for c in cs]
+    for copy in s_copies + nested + m_copies + p_copies:
         copy.wait_send()
     for copy in o_copies:
         copy.wait()
@@ -210,13 +248,20 @@
     bf16, f32 = jnp.bfloat16, jnp.float32
     dma = pltpu.SemaphoreType.DMA
     others = seqs - 1
+    parts = math.gcd(mine, PARTS)
     vmem = pl.BlockSpec(memory_space=pltpu.VMEM)
     return pl.pallas_call(
         functools.partial(kernel, seqs, chans, chunks),
         out_shape=jax.ShapeDtypeStruct((tok, cols), bf16),
-        in_specs=[vmem] * 5 + [pl.BlockSpec(memory_space=pl.ANY), vmem],
+        in_specs=[pl.BlockSpec(memory_space=pl.ANY)] * 7,
         out_specs=vmem,
         scratch_shapes=[
+            pltpu.VMEM((tok, width), bf16),
+            pltpu.VMEM((tok, width), bf16),
+            pltpu.VMEM((tok, width), bf16),
+            pltpu.VMEM((filts, length), bf16),
+            pltpu.VMEM((filts, length), bf16),
+            pltpu.VMEM((1, tok), jnp.int32),
             pltpu.VMEM((2, filts, length), f32),
             pltpu.VMEM((2, mine, TILE, length), bf16),
             pltpu.VMEM((seqs, rows, tok), bf16),
@@ -231,15 +276,16 @@
             pltpu.VMEM((chunks, tok, chunk), bf16),
             pltpu.VMEM((chunks, tok, chunk), bf16),
             pltpu.VMEM((chips, chunks, tok, chunk), bf16),
+            dma((6,)),
             dma((CORES, chunks)),
-            dma((others,)), dma((others,)), dma((others,)), dma((others,)),
-            dma((others,)), dma((others,)), dma((others,)), dma((others,)),
+            dma((parts, others)), dma((parts, others)), dma((parts, others)), dma((parts, others)),
+            dma((others,)), dma((others,)), dma((parts, others)), dma((parts, others)),
             dma((chunks,)), dma((chunks,)),
             dma((chunks, chips - 1)), dma((chunks, chips - 1)),
             dma((chunks,)), dma((chunks,)),
         ],
         compiler_params=pltpu.CompilerParams(
-            collective_id=0, has_side_effects=True, vmem_limit_bytes=48 * 1024 * 1024
+            collective_id=0, has_side_effects=True, vmem_limit_bytes=58 * 1024 * 1024
         ),
     )(value, gate1, gate2, filt1, filt2, weight, segs.reshape(1, tok))
 

time: 49.2 us -> 45.5 us (0.925)
  local copies, waits for them, and re-layouts: 6.15 us -> 2.29 us
    unnamed x13 -> x1, local copies, waits for them, and re-layouts: 6.15 us -> 2.29 us
where the time goes in v2:
time: 45.5 us; the launch traced here: 45.4 us
  Pallas kernels  43.1 us (95%)
  local copies, waits for them, and re-layouts  2.29 us (5%)
    pallas_call x1, Pallas kernels, local(): pl.pallas_call(functools.partial(kernel, seqs, chans, chunks), out_shape=...  43.1 us
    unnamed x1, local copies, waits for them, and re-layouts  2.29 us

profile of v2, /device:TPU:0, one launch (start us, length us, event | category | flops | bytes accessed | tf_op | source)
XLA Modules:
  0.0 45.4 jit_solution(7067626347200803100)
XLA Ops:
  0.0 43.1 %shard_map.73 = bf16[128,4096]{1,0:T(8,128)(2,1)} custom-call(bf16[128,1024]{1,0:T(8,128)(2,1)} %value_in.1, bf16[128,1024]{1,0:T(8,128)(2,1)} %gate1_in.1, bf16[128,1024]{1,0:T(8,128)(2,1)} %gate2_in.1, bf16[64,512]{1,0:T(8,128)(2,1)} %filt1_in.1, bf16[64,512]{1,0:T(8,128)(2,1)} %filt2_in.1, bf16[1024,4096]{1,0:T(8,128)(2,1)} %weight.1, s32[1,128]{1,0:T(1,128)} %bitcast.1), custom_call_target="tpu_custom_call" | custom-call | tf_op jit(solution)/shard_map/pallas_call | solution.py:253
  43.1 2.3 %copy.9 = bf16[128,4096]{1,0:T(8,128)(2,1)} copy(bf16[128,4096]{1,0:T(8,128)(2,1)} %shard_map.73) | data formatting | bytes 2097152

commit v3 on v2

--- a/solution.py
+++ b/solution.py
@@ -14,6 +14,7 @@
 CORES = 2
 GROUP = 4
 PARTS = 2
+HALVES = 2
 
 
 def remote(src, dst, send, recv, where):
@@ -27,7 +28,7 @@
     value_in, gate1_in, gate2_in, filt1_in, filt2_in, weight, segs_in,
     out,
     value, gate1, gate2, filt1, filt2, segs,
-    taps_f32, taps, z_send, z_recv, g_send, g_recv, seg_all, mix, m_send, m_recv,
+    taps_f32, taps, z_send, z_recv, g_send, g_recv, seg_all, mix, m_cols, m_send, m_recv,
     w_buf, p_send, p_recv, x_buf,
     i_sem, w_sem, z_ss, z_rs, g_ss, g_rs, s_ss, s_rs, m_ss, m_rs, p_ss, p_rs, x_ss, x_rs, o_ss, o_rs,
 ):
@@ -179,10 +180,22 @@
         results = [conv(1, f, field).astype(jnp.bfloat16) for f, field in zip(at, fields)]
         for f, result in zip(at, results):
             for j in range(seqs):
-                m_send[j, rows_of(f), :] = result[:, j * tok : (j + 1) * tok]
+                m_cols[j, rows_of(f), :] = result[:, j * tok : (j + 1) * tok]
         return carry
 
-    m_copies = []
+    sub = tok // HALVES
+    m_copies = [[] for _ in range(HALVES)]
+
+    def send_mixed(part, half):
+        span = pl.ds(half * sub, sub)
+        for d, peer in enumerate(seq_peers):
+            copy = remote(
+                m_send.at[part, peer, span], m_recv.at[part, me, span],
+                m_ss.at[part, half, d], m_rs.at[part, half, d], {"seq": peer},
+            )
+            copy.start()
+            m_copies[half].append(copy)
+
     for part in range(parts):
         base = part * part_filts
         for copy in z_copies[part]:
@@ -193,44 +206,65 @@
         for copy in g_copies[part]:
             copy.wait_recv()
         lax.fori_loop(0, part_filts // step, functools.partial(second_conv, base), 0)
-        m_copies += exchange(m_send, m_recv, m_ss, m_rs, part)
-    m_recv[me] = m_send[me]
+        span = pl.ds(part * part_rows, part_rows)
+        for j in range(seqs):
+            m_send[part, j] = m_cols[j, span, :].T
+        send_mixed(part, 0)
+    for half in range(1, HALVES):
+        for part in range(parts):
+            send_mixed(part, half)
+    for part in range(parts):
+        m_recv[part, me] = m_send[part, me]
     for copy in w_copies:
         copy.wait()
-    for copy in m_copies:
-        copy.wait_recv()
-
-    lhs = m_recv[...].reshape(seqs * rows, tok).T
-    p_copies = []
-    for q in range(chunks):
-        p_send[q] = jnp.dot(lhs, w_buf[0, q], preferred_element_type=jnp.float32).astype(jnp.bfloat16)
-        copy = remote(p_send.at[q], p_recv.at[q], p_ss.at[q], p_rs.at[q], {"chan": partner})
+    p_copies, x_copies, o_copies = [], [], []
+
+    def others_columns(lhs, half, q):
+        i = half * chunks + q
+        p_send[i] = jnp.dot(lhs, w_buf[0, q], preferred_element_type=jnp.float32).astype(jnp.bfloat16)
+        copy = remote(p_send.at[i], p_recv.at[i], p_ss.at[i], p_rs.at[i], {"chan": partner})
         copy.start()
         p_copies.append(copy)
-    x_copies = []
-    for q in range(chunks):
+
+    def my_columns(lhs, half, q):
+        i = half * chunks + q
         part = jnp.dot(lhs, w_buf[1, q], preferred_element_type=jnp.float32)
-        p_copies[q].wait_recv()
-        x_buf[chip, q] = (part + p_recv[q].astype(jnp.float32)).astype(jnp.bfloat16)
+        p_copies[i].wait_recv()
+        x_buf[chip, i] = (part + p_recv[i].astype(jnp.float32)).astype(jnp.bfloat16)
         x_copies.append([])
         for d, peer in enumerate(chip_peers):
-            copy = remote(x_buf.at[chip, q], x_buf.at[chip, q], x_ss.at[q, d], x_rs.at[q, d], {"chan": peer})
-            copy.start()
-            x_copies[q].append(copy)
-    o_copies = []
-    for q in range(chunks):
-        for copy in x_copies[q]:
+            copy = remote(x_buf.at[chip, i], x_buf.at[chip, i], x_ss.at[i, d], x_rs.at[i, d], {"chan": peer})
+            copy.start()
+            x_copies[i].append(copy)
+
+    for half in range(HALVES):
+        for copy in m_copies[half]:
             copy.wait_recv()
-        total = x_buf[0, q].astype(jnp.float32)
-        for j in range(1, chips):
-            total = total + x_buf[j, q].astype(jnp.float32)
-        here = out.at[:, pl.ds(pl.multiple_of(core * half_cols + q * width, width), width)]
-        here[...] = total.astype(jnp.bfloat16)
-        copy = remote(here, here, o_ss.at[q], o_rs.at[q], {"chan": partner})
-        copy.start()
-        o_copies.append(copy)
-    nested = [c for cs in z_copies + g_copies + x_copies for c in cs]
-    for copy in s_copies + nested + m_copies + p_copies:
+        span = slice(half * sub, (half + 1) * sub)
+        lhs = jnp.concatenate(
+            [m_recv[part, j, span, :] for j in range(seqs) for part in range(parts)], axis=1
+        )
+        others_columns(lhs, half, 0)
+        for q in range(chunks):
+            if q + 1 < chunks:
+                others_columns(lhs, half, q + 1)
+            my_columns(lhs, half, q)
+    for half in range(HALVES):
+        for q in range(chunks):
+            i = half * chunks + q
+            for copy in x_copies[i]:
+                copy.wait_recv()
+            total = x_buf[0, i].astype(jnp.float32)
+            for j in range(1, chips):
+                total = total + x_buf[j, i].astype(jnp.float32)
+            cols = pl.ds(pl.multiple_of(core * half_cols + q * width, width), width)
+            here = out.at[pl.ds(half * sub, sub), cols]
+            here[...] = total.astype(jnp.bfloat16)
+            copy = remote(here, here, o_ss.at[i], o_rs.at[i], {"chan": partner})
+            copy.start()
+            o_copies.append(copy)
+    nested = [c for cs in z_copies + g_copies + m_copies + x_copies for c in cs]
+    for copy in s_copies + nested + p_copies:
         copy.wait_send()
     for copy in o_copies:
         copy.wait()
@@ -248,12 +282,13 @@
     bf16, f32 = jnp.bfloat16, jnp.float32
     dma = pltpu.SemaphoreType.DMA
     others = seqs - 1
+    pieces = HALVES * chunks
     parts = math.gcd(mine, PARTS)
     vmem = pl.BlockSpec(memory_space=pltpu.VMEM)
     return pl.pallas_call(
         functools.partial(kernel, seqs, chans, chunks),
         out_shape=jax.ShapeDtypeStruct((tok, cols), bf16),
-        in_specs=[pl.BlockSpec(memory_space=pl.ANY)] * 7,
+        in_specs=[pl.BlockSpec(memory_space=pltpu.HBM)] * 7,
         out_specs=vmem,
         scratch_shapes=[
             pltpu.VMEM((tok, width), bf16),
@@ -271,18 +306,19 @@
             pltpu.VMEM((seqs, 1, tok), jnp.int32),
             pltpu.VMEM((rows, length), f32),
             pltpu.VMEM((seqs, rows, tok), bf16),
-            pltpu.VMEM((seqs, rows, tok), bf16),
+            pltpu.VMEM((parts, seqs, tok, rows // parts), bf16),
+            pltpu.VMEM((parts, seqs, tok, rows // parts), bf16),
             pltpu.VMEM((CORES, chunks, width, chunk), bf16),
-            pltpu.VMEM((chunks, tok, chunk), bf16),
-            pltpu.VMEM((chunks, tok, chunk), bf16),
-            pltpu.VMEM((chips, chunks, tok, chunk), bf16),
+            pltpu.VMEM((pieces, tok // HALVES, chunk), bf16),
+            pltpu.VMEM((pieces, tok // HALVES, chunk), bf16),
+            pltpu.VMEM((chips, pieces, tok // HALVES, chunk), bf16),
             dma((6,)),
             dma((CORES, chunks)),
             dma((parts, others)), dma((parts, others)), dma((parts, others)), dma((parts, others)),
-            dma((others,)), dma((others,)), dma((parts, others)), dma((parts, others)),
-            dma((chunks,)), dma((chunks,)),
-            dma((chunks, chips - 1)), dma((chunks, chips - 1)),
-            dma((chunks,)), dma((chunks,)),
+            dma((others,)), dma((others,)), dma((parts, HALVES, others)), dma((parts, HALVES, others)),
+            dma((pieces,)), dma((pieces,)),
+            dma((pieces, chips - 1)), dma((pieces, chips - 1)),
+            dma((pieces,)), dma((pieces,)),
         ],
         compiler_params=pltpu.CompilerParams(
             collective_id=0, has_side_effects=True, vmem_limit_bytes=58 * 1024 * 1024

time: 45.5 us -> 44.5 us (0.978)
  Pallas kernels: 43.1 us -> 42.1 us
    pallas_call x1, Pallas kernels: 43.1 us -> 42.1 us  [local(): pl.pallas_call(functools.partial(kernel, seqs, chans, chunks), out_shape=...]
where the time goes in v3:
time: 44.5 us; the launch traced here: 44.4 us
  Pallas kernels  42.1 us (95%)
  local copies, waits for them, and re-layouts  2.29 us (5%)
    pallas_call x1, Pallas kernels, local(): pl.pallas_call(functools.partial(kernel, seqs, chans, chunks), out_shape=...  42.1 us
    unnamed x1, local copies, waits for them, and re-layouts  2.29 us

profile of v3, /device:TPU:0, one launch (start us, length us, event | category | flops | bytes accessed | tf_op | source)
XLA Modules:
  0.0 44.4 jit_solution(6577461922919493925)
XLA Ops:
  0.0 42.1 %shard_map.73 = bf16[128,4096]{1,0:T(8,128)(2,1)} custom-call(bf16[128,1024]{1,0:T(8,128)(2,1)} %value_in.1, bf16[128,1024]{1,0:T(8,128)(2,1)} %gate1_in.1, bf16[128,1024]{1,0:T(8,128)(2,1)} %gate2_in.1, bf16[64,512]{1,0:T(8,128)(2,1)} %filt1_in.1, bf16[64,512]{1,0:T(8,128)(2,1)} %filt2_in.1, bf16[1024,4096]{1,0:T(8,128)(2,1)} %weight.1, s32[1,128]{1,0:T(1,128)} %bitcast.1), custom_call_target="tpu_custom_call" | custom-call | tf_op jit(solution)/shard_map/pallas_call | solution.py:288
  42.1 2.3 %copy.9 = bf16[128,4096]{1,0:T(8,128)(2,1)} copy(bf16[128,4096]{1,0:T(8,128)(2,1)} %shard_map.73) | data formatting | bytes 2097152

commit v4 on v3

--- a/solution.py
+++ b/solution.py
@@ -15,6 +15,7 @@
 GROUP = 4
 PARTS = 2
 HALVES = 2
+STRIP = 16
 
 
 def remote(src, dst, send, recv, where):
@@ -29,8 +30,8 @@
     out,
     value, gate1, gate2, filt1, filt2, segs,
     taps_f32, taps, z_send, z_recv, g_send, g_recv, seg_all, mix, m_cols, m_send, m_recv,
-    w_buf, p_send, p_recv, x_buf,
-    i_sem, w_sem, z_ss, z_rs, g_ss, g_rs, s_ss, s_rs, m_ss, m_rs, p_ss, p_rs, x_ss, x_rs, o_ss, o_rs,
+    w_buf, p_send, p_recv, x_buf, o_buf,
+    i_sem, w_sem, z_ss, z_rs, g_ss, g_rs, s_ss, s_rs, m_ss, m_rs, p_ss, p_rs, x_ss, x_rs, o_ss, o_rs, o_ls,
 ):
     me = lax.axis_index("seq")
     chan = lax.axis_index("chan")
@@ -259,14 +260,28 @@
                 total = total + x_buf[j, i].astype(jnp.float32)
             cols = pl.ds(pl.multiple_of(core * half_cols + q * width, width), width)
             here = out.at[pl.ds(half * sub, sub), cols]
-            here[...] = total.astype(jnp.bfloat16)
-            copy = remote(here, here, o_ss.at[i], o_rs.at[i], {"chan": partner})
+            o_buf[i] = total.astype(jnp.bfloat16)
+            copy = pltpu.make_async_copy(o_buf.at[i], here, o_ls.at[i])
+            copy.start()
+            o_copies.append(copy)
+            copy = remote(o_buf.at[i], here, o_ss.at[i], o_rs.at[i], {"chan": partner})
             copy.start()
             o_copies.append(copy)
     nested = [c for cs in z_copies + g_copies + m_copies + x_copies for c in cs]
     for copy in s_copies + nested + p_copies:
         copy.wait_send()
     for copy in o_copies:
+        copy.wait()
+
+
+def hand_on(source, target, sems):
+    copies = []
+    for i in range(source.shape[0] // STRIP):
+        span = pl.ds(i * STRIP, STRIP)
+        copy = pltpu.make_async_copy(source.at[span], target.at[span], sems.at[i])
+        copy.start()
+        copies.append(copy)
+    for copy in copies:
         copy.wait()
 
 
@@ -284,12 +299,12 @@
     others = seqs - 1
     pieces = HALVES * chunks
     parts = math.gcd(mine, PARTS)
-    vmem = pl.BlockSpec(memory_space=pltpu.VMEM)
-    return pl.pallas_call(
+    hbm = pl.BlockSpec(memory_space=pltpu.HBM)
+    mixed = pl.pallas_call(
         functools.partial(kernel, seqs, chans, chunks),
         out_shape=jax.ShapeDtypeStruct((tok, cols), bf16),
-        in_specs=[pl.BlockSpec(memory_space=pltpu.HBM)] * 7,
-        out_specs=vmem,
+        in_specs=[hbm] * 7,
+        out_specs=hbm,
         scratch_shapes=[
             pltpu.VMEM((tok, width), bf16),
             pltpu.VMEM((tok, width), bf16),
@@ -312,18 +327,26 @@
             pltpu.VMEM((pieces, tok // HALVES, chunk), bf16),
             pltpu.VMEM((pieces, tok // HALVES, chunk), bf16),
             pltpu.VMEM((chips, pieces, tok // HALVES, chunk), bf16),
+            pltpu.VMEM((pieces, tok // HALVES, chunk), bf16),
             dma((6,)),
             dma((CORES, chunks)),
             dma((parts, others)), dma((parts, others)), dma((parts, others)), dma((parts, others)),
             dma((others,)), dma((others,)), dma((parts, HALVES, others)), dma((parts, HALVES, others)),
             dma((pieces,)), dma((pieces,)),
             dma((pieces, chips - 1)), dma((pieces, chips - 1)),
-            dma((pieces,)), dma((pieces,)),
+            dma((pieces,)), dma((pieces,)), dma((pieces,)),
         ],
         compiler_params=pltpu.CompilerParams(
             collective_id=0, has_side_effects=True, vmem_limit_bytes=58 * 1024 * 1024
         ),
     )(value, gate1, gate2, filt1, filt2, weight, segs.reshape(1, tok))
+    return pl.pallas_call(
+        hand_on,
+        out_shape=jax.ShapeDtypeStruct((tok, cols), bf16),
+        in_specs=[hbm],
+        out_specs=hbm,
+        scratch_shapes=[dma((tok // STRIP,))],
+    )(mixed)
 
 
 def solution(mesh):

time: 44.5 us -> 74.4 us (1.67)
  Pallas kernels: 42.1 us -> 74.2 us
  local copies, waits for them, and re-layouts: 2.29 us -> 0 us
    pallas_call x0 -> x1, Pallas kernels: none -> 32.9 us  [local(): pl.pallas_call(hand_on, out_shape=jax.ShapeDtypeStruct((tok, cols), bf16)...]
    unnamed x1 -> x0, local copies, waits for them, and re-layouts: 2.29 us -> none
    pallas_call x1, Pallas kernels: 42.1 us -> 41.3 us  [local(): pl.pallas_call(functools.partial(kernel, seqs, chans, chunks), out_shape=...]
where the time goes in v4:
time: 74.4 us; the launch traced here: 74.3 us
  Pallas kernels  74.2 us (100%)
    pallas_call x1, Pallas kernels, local(): pl.pallas_call(functools.partial(kernel, seqs, chans, chunks), out_shape=...  41.3 us
    pallas_call x1, Pallas kernels, local(): pl.pallas_call(hand_on, out_shape=jax.ShapeDtypeStruct((tok, cols), bf16)...  32.9 us

profile of v4, /device:TPU:0, one launch (start us, length us, event | category | flops | bytes accessed | tf_op | source)
XLA Modules:
  0.0 74.3 jit_solution(5305755917824381229)
XLA Ops:
  0.0 41.3 %shard_map.73.source = bf16[128,4096]{1,0:T(8,128)(2,1)} custom-call(bf16[128,1024]{1,0:T(8,128)(2,1)} %value_in.1, bf16[128,1024]{1,0:T(8,128)(2,1)} %gate1_in.1, bf16[128,1024]{1,0:T(8,128)(2,1)} %gate2_in.1, bf16[64,512]{1,0:T(8,128)(2,1)} %filt1_in.1, bf16[64,512]{1,0:T(8,128)(2,1)} %filt2_in.1, bf16[1024,4096]{1,0:T(8,128)(2,1)} %weight.1, s32[1,128]{1,0:T(1,128)} %bitcast.1), custom_call_target="tpu_custom_call" | custom-call | tf_op jit(solution)/shard_map/pallas_call | solution.py:303
  41.3 32.9 %shard_map.74 = bf16[128,4096]{1,0:T(8,128)(2,1)} custom-call(bf16[128,4096]{1,0:T(8,128)(2,1)} %shard_map.73.source), custom_call_target="tpu_custom_call" | custom-call | tf_op jit(solution)/shard_map/pallas_call | solution.py:343

commit v5 on v4

--- a/solution.py
+++ b/solution.py
@@ -274,14 +274,20 @@
         copy.wait()
 
 
-def hand_on(source, target, sems):
-    copies = []
+def hand_on(source, target, held, in_sems, out_sems):
+    arriving, leaving = [], []
     for i in range(source.shape[0] // STRIP):
         span = pl.ds(i * STRIP, STRIP)
-        copy = pltpu.make_async_copy(source.at[span], target.at[span], sems.at[i])
-        copy.start()
-        copies.append(copy)
-    for copy in copies:
+        copy = pltpu.make_async_copy(source.at[span], held.at[span], in_sems.at[i])
+        copy.start()
+        arriving.append(copy)
+    for i, copy in enumerate(arriving):
+        span = pl.ds(i * STRIP, STRIP)
+        copy.wait()
+        copy = pltpu.make_async_copy(held.at[span], target.at[span], out_sems.at[i])
+        copy.start()
+        leaving.append(copy)
+    for copy in leaving:
         copy.wait()
 
 
@@ -345,7 +351,7 @@
         out_shape=jax.ShapeDtypeStruct((tok, cols), bf16),
         in_specs=[hbm],
         out_specs=hbm,
-        scratch_shapes=[dma((tok // STRIP,))],
+        scratch_shapes=[pltpu.VMEM((tok, cols), bf16), dma((tok // STRIP,)), dma((tok // STRIP,))],
     )(mixed)
 
 

time: 74.4 us -> 43.5 us (0.58)
  Pallas kernels: 74.2 us -> 43.4 us
    pallas_call x1, Pallas kernels: 32.9 us -> 2.09 us  [local(): pl.pallas_call(hand_on, out_shape=jax.ShapeDtypeStruct((tok, cols), bf16)...]
where the time goes in v5:
time: 43.5 us; the launch traced here: 43.4 us
  Pallas kernels  43.4 us (100%)
    pallas_call x1, Pallas kernels, local(): pl.pallas_call(functools.partial(kernel, seqs, chans, chunks), out_shape=...  41.3 us
    pallas_call x1, Pallas kernels, local(): pl.pallas_call(hand_on, out_shape=jax.ShapeDtypeStruct((tok, cols), bf16)...  2.09 us

profile of v5, /device:TPU:0, one launch (start us, length us, event | category | flops | bytes accessed | tf_op | source)
XLA Modules:
  0.0 43.4 jit_solution(14765720160257235167)
XLA Ops:
  0.0 41.3 %shard_map.73.source = bf16[128,4096]{1,0:T(8,128)(2,1)} custom-call(bf16[128,1024]{1,0:T(8,128)(2,1)} %value_in.1, bf16[128,1024]{1,0:T(8,128)(2,1)} %gate1_in.1, bf16[128,1024]{1,0:T(8,128)(2,1)} %gate2_in.1, bf16[64,512]{1,0:T(8,128)(2,1)} %filt1_in.1, bf16[64,512]{1,0:T(8,128)(2,1)} %filt2_in.1, bf16[1024,4096]{1,0:T(8,128)(2,1)} %weight.1, s32[1,128]{1,0:T(1,128)} %bitcast.1), custom_call_target="tpu_custom_call" | custom-call | tf_op jit(solution)/shard_map/pallas_call | solution.py:309
  41.3 2.1 %shard_map.74 = bf16[128,4096]{1,0:T(8,128)(2,1)} custom-call(bf16[128,4096]{1,0:T(8,128)(2,1)} %shard_map.73.source), custom_call_target="tpu_custom_call" | custom-call | tf_op jit(solution)/shard_map/pallas_call | solution.py:349
